TPU v7x, 128 devices: a whole 4x4x4 slice. The times are simulated.
128 devices in a mesh: rep: 8 (over x, core), graph: 16 (over y, z).
Axes of the slice: x: 4, y: 4, z: 4, core: 2. Of those that a mesh axis runs over, the one named last changes fastest.
Arguments:
- node_feats: bfloat16 [4096, 49, 128], P(('rep', 'graph')), may hold values from -6 to 6
- grad_out: bfloat16 [4096, 49, 128], P(('rep', 'graph')), may hold values from -6 to 6
- wigner: bfloat16 [235, 81920], P(None, ('rep', 'graph')), may hold values from -1.796875 to 1.796875
- weight_zero: bfloat16 [896, 896], replicated, may hold values from -0.1875 to 0.1875
- weight_one: bfloat16 [768, 2, 768], replicated, may hold values from -0.15625 to 0.15625
- weight_two: bfloat16 [640, 2, 640], replicated, may hold values from -0.15625 to 0.15625
- edge_source: int32 [81920], P(('rep', 'graph')), may hold values from 0 to 511
- edge_target: int32 [81920], P(('rep', 'graph')), may hold values from 0 to 31
- edge_count: int32 [128], P(('rep', 'graph')), may hold values from 320 to 640, as said below
Outputs:
- grad_feats: bfloat16 [4096, 49, 128], P(('rep', 'graph'))
- grad_zero: float32 [896, 896], P('graph')
- grad_one: float32 [768, 2, 768], P('graph')
- grad_two: float32 [640, 2, 640], P('graph')
Inputs may be any that keep to these rules, and one draw needn't show every extreme that they name: `edge_count`: at least half of a device's 640 slots are live, and some device has all 640 live.
All inputs are finite; a program needn't handle non-finite values.
Results may differ from a plain program's by a relative error of at most 0.015.
Values may be sent and summed in bfloat16 or wider, within the bound.
No kernel may reach another device: no remote copies, remote signals or barrier semaphores. Data moves between devices by JAX's collectives and lax.ppermute only.
A program may use at most 192 MiB of HBM per device.

v0:
```python
import jax
import jax.numpy as jnp
from jax import lax
from jax.experimental import pallas as pl
from jax.experimental.pallas import tpu as pltpu
from jax.sharding import PartitionSpec as P

LMAX = 6
C = 128
FIRST_TILES = ((0, 5), (0, 6), (0, 5))
SECOND_TILES = ((5, 7), (6, 12), (5, 10))
FIRST_ROWS, SECOND_ROWS = 96, 80
F32, BF16 = jnp.float32, jnp.bfloat16


def rot_offset(l):
    return sum((2 * min(i, 2) + 1) * (2 * i + 1) for i in range(l))


def rows_of(l):
    return 2 * min(l, 2) + 1


CH = 64
PARTS_STEP = 8


def turn(l, edges, rot_ref, in_ref, emit, loop=False):
    kept, full, first = rows_of(l), 2 * l + 1, rot_offset(l)

    def one(e0):
        for c0 in range(0, C, CH):
            acc = [None] * kept
            for n in range(full):
                x = in_ref[pl.ds(n * C + c0, CH), pl.ds(e0, 128)]
                for r in range(kept):
                    f = rot_ref[pl.ds(first + r * full + n, 1), pl.ds(e0, 128)]
                    t = f * x
                    acc[r] = t if acc[r] is None else acc[r] + t
            for r in range(kept):
                emit(r, c0, e0, acc[r])

    if loop:

        @pl.loop(0, edges // 128)
        def _(tile):
            one(pl.multiple_of(tile * 128, 128))
    else:
        for tile in range(edges // 128):
            one(tile * 128)


def nt(a, b):
    return lax.dot_general(a, b, (((1,), (1,)), ((), ())), preferred_element_type=F32)


def tn(a, b):
    return lax.dot_general(a, b, (((0,), (0,)), ((), ())), preferred_element_type=F32)


def grad_kernel(count_ref, g_ref, wig_ref, w0_ref, w1_ref, w2_ref, src_ref, tgt_ref,
                g0_ref, g1_ref, g2_ref, part_ref,
                rot_ref, rows_ref, gv0_ref, gv1_ref, gv2_ref, gx_ref, own_ref):
    edges = wig_ref.shape[1]
    atoms = g_ref.shape[1]
    parts = part_ref.shape[0]
    rot_ref[...] = wig_ref[...].astype(F32)
    slot = lax.broadcasted_iota(jnp.int32, (atoms, edges), 1)
    atom = lax.broadcasted_iota(jnp.int32, (atoms, edges), 0)
    chosen = jnp.where((tgt_ref[...] == atom) & (slot < count_ref[0]), 1.0, 0.0).astype(BF16)
    for l in range(LMAX + 1):
        kept, full = rows_of(l), 2 * l + 1
        half = kept // 2
        g = jnp.concatenate([g_ref[l * l + n] for n in range(full)], axis=1)
        rows_ref[: full * C, :] = tn(g, chosen)

        def emit(r, c0, e0, value, l=l, half=half):
            m = r - half
            v = value.astype(BF16)
            if m == 0:
                g0_ref[pl.ds(l * C + c0, CH), pl.ds(e0, 128)] = v
                return
            ref = g1_ref if abs(m) == 1 else g2_ref
            deep = ref.shape[0] // 2
            at = (l - abs(m)) * C + c0
            if m > 0:
                ref[pl.ds(at, CH), pl.ds(e0, 128)] = v
                ref[pl.ds(deep + at, CH), pl.ds(edges + e0, 128)] = -v
            else:
                ref[pl.ds(deep + at, CH), pl.ds(e0, 128)] = v
                ref[pl.ds(at, CH), pl.ds(edges + e0, 128)] = v

        turn(l, edges, rot_ref, rows_ref, emit, True)
    gv0_ref[...] = jnp.dot(w0_ref[...], g0_ref[...], preferred_element_type=F32).astype(BF16).astype(F32)

    @pl.loop(0, 2)
    def _(k):
        at = pl.ds(pl.multiple_of(k * edges, 128), edges)
        gv1_ref[:, at] = jnp.dot(w1_ref[...], g1_ref[:, at], preferred_element_type=F32).astype(BF16).astype(F32)
        gv2_ref[:, at] = jnp.dot(w2_ref[...], g2_ref[:, at], preferred_element_type=F32).astype(BF16).astype(F32)
    atom = lax.broadcasted_iota(jnp.int32, (parts * atoms, edges), 0)
    own_ref[...] = jnp.where(src_ref[...] == atom, 1.0, 0.0).astype(BF16)
    for l in range(LMAX + 1):
        kept, full, first = rows_of(l), 2 * l + 1, rot_offset(l)
        half = kept // 2

        @pl.loop(0, edges // 128)
        def _(tile):
            e0 = pl.multiple_of(tile * 128, 128)
            for c0 in range(0, C, CH):
                s = []
                for r in range(kept):
                    m = r - half
                    ref = (gv0_ref, gv1_ref, gv2_ref)[abs(m)]
                    s.append(ref[pl.ds((l - abs(m)) * C + c0, CH), pl.ds((edges if m < 0 else 0) + e0, 128)])
                for n in range(full):
                    acc = None
                    for r in range(kept):
                        f = rot_ref[pl.ds(first + r * full + n, 1), pl.ds(e0, 128)]
                        t = f * s[r]
                        acc = t if acc is None else acc + t
                    gx_ref[pl.ds(n * C + c0, CH), pl.ds(e0, 128)] = acc.astype(BF16)


        @pl.loop(0, parts // PARTS_STEP)
        def _(step):
            rows = PARTS_STEP * atoms
            out = nt(own_ref[pl.ds(pl.multiple_of(step * rows, rows), rows), :], gx_ref[: full * C, :]).astype(BF16)
            for n in range(full):
                part_ref[pl.ds(step * PARTS_STEP, PARTS_STEP), l * l + n] = out[:, n * C : (n + 1) * C].reshape(
                    PARTS_STEP, atoms, C
                )


def products(place_ref, v_refs, g_refs, tiles, slab_ref, mine_refs, their_ref):
    parts = slab_ref.shape[0]
    base = 0
    for v_ref, g_ref, (begin, end) in zip(v_refs, g_refs, tiles):
        share = v_ref.shape[0] // parts
        for j in range(begin * C, end * C, 256):
            wide = min(256, end * C - j)
            d = nt(v_ref[...], g_ref[j : j + wide, :])
            for k in range(0, wide, C):
                slab_ref[:, base : base + share, :] = d[:, k : k + C].reshape(parts, share, C)
                base += share
    if base < slab_ref.shape[1]:
        slab_ref[:, base:, :] = jnp.zeros((parts, slab_ref.shape[1] - base, C), F32)
    part_rows = mine_refs[0].shape[1]
    x, core = place_ref[0], place_ref[1]
    for k in range(4):
        group = 2 * lax.rem(x + k, 4)
        at = pl.ds(pl.multiple_of((group + core) * part_rows, 8), part_rows)
        mine_refs[k][...] = slab_ref[:, at, :].astype(BF16)
        at = pl.ds(pl.multiple_of((group + 1 - core) * part_rows, 8), part_rows)
        their_ref[k] = slab_ref[:, at, :].astype(BF16)


def first_kernel(place_ref, x_hbm, g1_hbm, g2_hbm, wig_ref, src_ref, g0_ref,
                 v0_ref, v1_ref, v2_ref, mine0, mine1, mine2, mine3, their_ref,
                 x_ref, g1_ref, g2_ref, sems, rot_ref, rows_ref, slab_ref):
    parts, _, atoms, _ = x_ref.shape
    edges = wig_ref.shape[1]
    copies = []
    for l in range(LMAX + 1):
        at = pl.ds(l * l, 2 * l + 1)
        copies.append(pltpu.make_async_copy(x_hbm.at[:, at], x_ref.at[:, at], sems.at[l]))
        copies[l].start()
    for k, (hbm, ref) in enumerate(((g1_hbm, g1_ref), (g2_hbm, g2_ref))):
        copies.append(pltpu.make_async_copy(hbm, ref, sems.at[LMAX + 1 + k]))
        copies[-1].start()
    rot_ref[...] = wig_ref[...].astype(F32)
    atom = lax.broadcasted_iota(jnp.int32, (parts * atoms, edges), 0)
    chosen = jnp.where(src_ref[...] == atom, 1.0, 0.0).astype(BF16)
    for l in range(LMAX + 1):
        kept, full = rows_of(l), 2 * l + 1
        half = kept // 2
        copies[l].wait()
        x = jnp.concatenate([x_ref[:, l * l + n].reshape(parts * atoms, C) for n in range(full)], axis=1)
        rows_ref[: full * C, :] = tn(x, chosen)

        def emit(r, c0, e0, value, l=l, half=half):
            m = r - half
            ref = (v0_ref, v1_ref, v2_ref)[abs(m)]
            ref[pl.ds((l - abs(m)) * C + c0, CH), pl.ds((edges if m < 0 else 0) + e0, 128)] = value.astype(BF16)

        turn(l, edges, rot_ref, rows_ref, emit)
    for copy in copies[LMAX + 1 :]:
        copy.wait()
    products(place_ref, (v0_ref, v1_ref, v2_ref), (g0_ref, g1_ref, g2_ref), FIRST_TILES, slab_ref,
             (mine0, mine1, mine2, mine3), their_ref)


def second_kernel(place_ref, v0_ref, v1_ref, v2_ref, g0_ref, g1_ref, g2_ref,
                  mine0, mine1, mine2, mine3, their_ref, slab_ref):
    products(place_ref, (v0_ref, v1_ref, v2_ref), (g0_ref, g1_ref, g2_ref), SECOND_TILES, slab_ref,
             (mine0, mine1, mine2, mine3), their_ref)


VM = pl.BlockSpec(memory_space=pltpu.VMEM)
SM = pl.BlockSpec(memory_space=pltpu.SMEM)
ANY = pl.BlockSpec(memory_space=pltpu.HBM)
S = jax.ShapeDtypeStruct


def grads(count, g, wig, w0, w1, w2, src, tgt, parts):
    coefs, atoms, _ = g.shape
    edges = wig.shape[1]
    rot = wig.shape[0]
    k0, k1, k2 = w0.shape[0], w1.shape[0], w2.shape[0]
    return pl.pallas_call(
        grad_kernel,
        out_shape=(S((k0, edges), BF16), S((2 * k1, 2 * edges), BF16), S((2 * k2, 2 * edges), BF16),
                   S((parts, coefs, atoms, C), BF16)),
        in_specs=[SM] + [VM] * 7,
        out_specs=[VM] * 4,
        scratch_shapes=[pltpu.VMEM((rot, edges), F32), pltpu.VMEM((13 * C, edges), F32),
                        pltpu.VMEM((k0, edges), F32), pltpu.VMEM((k1, 2 * edges), F32),
                        pltpu.VMEM((k2, 2 * edges), F32), pltpu.VMEM((13 * C, edges), BF16),
                        pltpu.VMEM((parts * atoms, edges), BF16)],
        compiler_params=pltpu.CompilerParams(vmem_limit_bytes=36 << 20),
        name="grads",
    )(count, g, wig, w0, w1, w2, src, tgt)


def sums(parts, rows):
    return tuple(S((parts, rows, C), BF16) for _ in range(4)) + (S((4, parts, rows, C), BF16),)


def first_weights(place, x, wig, src, g0, g1, g2):
    edges = wig.shape[1]
    rot = wig.shape[0]
    parts = x.shape[0]
    k0, k1, k2 = g0.shape[0], g1.shape[0] // 2, g2.shape[0] // 2
    return pl.pallas_call(
        first_kernel,
        out_shape=(S((k0, edges), BF16), S((k1, 2 * edges), BF16), S((k2, 2 * edges), BF16)) + sums(parts, FIRST_ROWS),
        in_specs=[SM, ANY, ANY, ANY] + [VM] * 3,
        out_specs=[VM] * 8,
        scratch_shapes=[pltpu.VMEM(x.shape, BF16), pltpu.VMEM(g1.shape, BF16), pltpu.VMEM(g2.shape, BF16),
                        pltpu.SemaphoreType.DMA((LMAX + 3,)),
                        pltpu.VMEM((rot, edges), F32), pltpu.VMEM((13 * C, edges), F32),
                        pltpu.VMEM((parts, 8 * FIRST_ROWS, C), F32)],
        compiler_params=pltpu.CompilerParams(vmem_limit_bytes=40 << 20),
        cost_estimate=pl.CostEstimate(flops=10_000_000_000, bytes_accessed=20_000_000, transcendentals=0),
        name="first_weights",
    )(place, x, g1, g2, wig, src, g0)


def second_weights(place, v0, v1, v2, g0, g1, g2, parts):
    return pl.pallas_call(
        second_kernel,
        out_shape=sums(parts, SECOND_ROWS),
        in_specs=[SM] + [VM] * 6,
        out_specs=[VM] * 5,
        scratch_shapes=[pltpu.VMEM((parts, 8 * SECOND_ROWS, C), F32)],
        compiler_params=pltpu.CompilerParams(vmem_limit_bytes=32 << 20),
        cost_estimate=pl.CostEstimate(flops=4_000_000_000, bytes_accessed=10_000_000, transcendentals=0),
        name="second_weights",
    )(place, v0, v1, v2, g0, g1, g2)


def graph_shift(dy, dz):
    return [(y * 4 + z, (y + dy) % 4 * 4 + (z + dz) % 4) for y in range(4) for z in range(4)]


def rep_shift(dx, dc):
    return [(x * 2 + c, (x + dx) % 4 * 2 + (c + dc) % 2) for x in range(4) for c in range(2)]


def send_rep(value, dx, dc):
    return lax.ppermute(value, "rep", rep_shift(dx, dc))


def add(*terms):
    total = terms[0].astype(F32)
    for t in terms[1:]:
        total = total + t.astype(F32)
    return total.astype(BF16)


def sum_over_rep(mine, theirs):
    got = send_rep(theirs, 0, 1)
    r = [add(mine[k], got[k]) for k in range(4)]
    half = r[2].shape[0] // 2
    up = send_rep(r[2][:half], 1, 0)
    down = send_rep(r[2][half:], -1, 0)
    r1 = jnp.concatenate([add(r[1][:half], up), r[1][half:]])
    r3 = jnp.concatenate([r[3][:half], add(r[3][half:], down)])
    return add(r[0], send_rep(r1, 1, 0), send_rep(r3, -1, 0))


def per_device(node_feats, grad_out, wigner, w0, w1, w2, edge_source, edge_target, edge_count):
    atoms, coefs, _ = node_feats.shape
    parts = lax.axis_size("graph")
    edges = edge_source.shape[0]
    x = lax.all_gather(node_feats.transpose(1, 0, 2), "graph", axis=0, tiled=False)
    src, tgt = edge_source[None], edge_target[None]
    g0, g1, g2, part = grads(
        edge_count, grad_out.transpose(1, 0, 2), wigner, w0, w1.reshape(w1.shape[0], -1), w2.reshape(w2.shape[0], -1), src, tgt, parts
    )
    grad_feats = lax.psum_scatter(part, "graph", scatter_dimension=0, tiled=False).transpose(1, 0, 2)
    rep = lax.axis_index("rep")
    place = jnp.stack([rep // 2, rep % 2])
    v0, v1, v2, *mine, theirs = first_weights(place, x, wigner, src, g0, g1, g2)
    first = sum_over_rep(mine, theirs)
    *mine, theirs = second_weights(place, v0, v1, v2, g0, g1, g2, parts)
    second = sum_over_rep(mine, theirs)
    pieces = lax.all_to_all(jnp.concatenate([first, second], axis=1), "graph", split_axis=0, concat_axis=0, tiled=True)
    whole = lax.all_gather(pieces.astype(F32).sum(0), "rep", axis=0, tiled=False)
    first = whole[:, :FIRST_ROWS].reshape(-1, C)
    second = whole[:, FIRST_ROWS:].reshape(-1, C)
    scale = float(lax.axis_size("rep") * parts * edges) ** (-0.5)
    outs = []
    first_at = second_at = 0
    for w, early, late in zip((w0, w1, w2), FIRST_TILES, SECOND_TILES):
        share = w.shape[0] // parts
        n, k = (early[1] - early[0]) * share, (late[1] - late[0]) * share
        rows = jnp.concatenate([first[first_at : first_at + n], second[second_at : second_at + k]])
        first_at, second_at = first_at + n, second_at + k
        rows = rows.reshape(-1, share, C).transpose(1, 0, 2)
        outs.append(rows.reshape((share,) + w.shape[1:]) * scale)
    return (grad_feats, *outs)


def solution(mesh):
    both = P(("rep", "graph"))
    edge_spec = P(("rep", "graph"))
    in_specs = (both, both, P(None, ("rep", "graph")), P(), P(), P(), edge_spec, edge_spec, edge_spec)
    out_specs = (both, P("graph"), P("graph"), P("graph"))
    return jax.shard_map(per_device, mesh=mesh, in_specs=in_specs, out_specs=out_specs, check_vma=False)
```

profile of v0, /device:TPU:1, one launch (start us, length us, event | category | flops | bytes accessed | tf_op | source)
XLA Modules:
  0.0 182.1 jit_solution(3714926579709982158)
XLA Ops:
  7.2 0.7 all-gather.4.cloned.1.call-update
  8.6 2.2 %copy.20 = bf16[96,8,2,768]{3,1,2,0:T(8,128)(2,1)S(1)} copy(bf16[96,8,2,768]{3,2,1,0:T(2,128)(2,1)} %bitcast.74) | data formatting | bytes 4718592
  10.9 0.3 copy.21
  11.2 0.4 copy-done.9
  11.5 0.7 copy-done
  12.4 34.7 %grads.1 = (bf16[896,640]{1,0:T(8,128)(2,1)S(1)}, bf16[1536,1280]{1,0:T(8,128)(2,1)S(1)}, bf16[1280,1280]{1,0:T(8,128)(2,1)S(1)}, bf16[16,49,32,128]{3,2,1,0:T(8,128)(2,1)}) custom-call(s32[1]{0:T(128)S(6)} %copy.24.count_ref, bf16[49,32,128]{2,1,0:T(8,128)(2,1)S(1)} %bitcast.71, bf16[235,640]{1,0:T(8,128)(2,1)S(1)} %copy-done.2, ...), custom_call_target="tpu_custom_call" | custom-call | tf_op jit(solution)/shard_map/grads/pallas_call | solution.py:210
  47.2 1.9 %copy-done.3 = bf16[1536,1280]{1,0:T(8,128)(2,1)} copy-done((bf16[1536,1280]{1,0:T(8,128)(2,1)}, bf16[1536,1280]{1,0:T(8,128)(2,1)S(1)}, u32[]{:S(2)}) %copy-start.3) | copy-done | bytes 3932184
  49.0 1.7 copy-done.5
  50.8 24.6 %all-gather.4.cloned.1.call-done = bf16[784,32,128]{2,1,0:T(8,128)(2,1)} async-done(((bf16[49,32,128]{2,1,0:T(8,128)(2,1)}), bf16[784,32,128]{2,1,0:T(8,128)(2,1)}) %all-gather.4.cloned.1.call-update) | async-done | bytes 6422544 | tf_op jit(solution)/shard_map/all_gather | solution.py:296
  75.4 1.9 %copy-done.6 = bf16[1280,1280]{1,0:T(8,128)(2,1)S(1)} copy-done((bf16[1280,1280]{1,0:T(8,128)(2,1)S(1)}, bf16[1280,1280]{1,0:T(8,128)(2,1)}, u32[]{:S(2)}) %copy-start.6) | copy-done | bytes 3276824
  77.3 18.0 %first_weights.1 = (bf16[896,640]{1,0:T(8,128)(2,1)S(1)}, bf16[768,1280]{1,0:T(8,128)(2,1)S(1)}, bf16[640,1280]{1,0:T(8,128)(2,1)S(1)}, bf16[16,96,128]{2,1,0:T(...) custom-call(s32[2]{0:T(128)S(1)} %pad_add_fusion.place_ref, ...), custom_call_target="tpu_custom_call" | custom-call | flops 10000000000 | bytes 20000000 | tf_op jit(solution)/shard_map/first_weights/pallas_call | solution.py:234
  95.4 4.1 %second_weights.1 = (bf16[16,80,128]{2,1,0:T(8,128)(2,1)S(1)}, bf16[16,80,128]{2,1,0:T(8,128)(2,1)S(1)}, bf16[16,80,128]{2,1,0:T(8,128)(2,1)S(1)}, bf16[16,80,12...) custom-call(s32[2]{0:T(128)S(1)} %pad_add_fusion.place_ref, bf16[896,640]{1,0:T(8,128)(2,1)S(1)} %get-tuple-element.30.v0_ref, ...), custom_call_target="tpu_custom_call" | custom-call | flops 4000000000 | bytes 10000000 | tf_op jit(solution)/shard_map/second_weights/pallas_call | solution.py:250
  99.6 0.8 collective-permute-start.5
  100.4 2.6 %collective-permute-done.5 = bf16[4,16,80,128]{3,2,1,0:T(8,128)(2,1)S(1)} collective-permute-done((bf16[4,16,80,128]{3,2,1,0:T(8,128)(2,1)S(1)}, bf16[4,16,80,128]{3,2,1,0:T(8,128)(2,1)S(1)}, u32[]{:S(2)}, u32[]{:S(2)}) %collective-permute-start.5) | collective-permute-done | bytes 1310752 | tf_op jit(solution)/shard_map/ppermute | solution.py:271
  103.0 0.3 fusion.6
  103.3 2.5 %collective-permute-start.8 = (bf16[8,80,128]{2,1,0:T(8,128)(2,1)S(1)}, bf16[8,80,128]{2,1,0:T(8,128)(2,1)S(1)}, u32[]{:S(2)}, u32[]{:S(2)}) collective-permute-start(bf16[8,80,128]{2,1,0:T(8,128)(2,1)S(1)} %get-tuple-element.47), channel_id=1, source_target_pairs={{0,96},{16,112},{32,0},{48,16},{64,32},{80,48},{96,64},{112,80},{1... | collective-permute-start | bytes 491528 | tf_op jit(solution)/shard_map/ppermute | solution.py:271
  105.9 3.1 %collective-permute-done.8 = bf16[8,80,128]{2,1,0:T(8,128)(2,1)S(1)} collective-permute-done((bf16[8,80,128]{2,1,0:T(8,128)(2,1)S(1)}, bf16[8,80,128]{2,1,0:T(8,128)(2,1)S(1)}, u32[]{:S(2)}, u32[]{:S(2)}) %collective-permute-start.8) | collective-permute-done | bytes 163872 | tf_op jit(solution)/shard_map/ppermute | solution.py:271
  109.0 3.6 %collective-permute-start.9 = (bf16[16,80,128]{2,1,0:T(8,128)(2,1)S(1)}, bf16[16,80,128]{2,1,0:T(8,128)(2,1)S(1)}, u32[]{:S(2)}, u32[]{:S(2)}) collective-permute-start(bf16[16,80,128]{2,1,0:T(8,128)(2,1)S(1)} %pad_maximum_fusion.4), channel_id=1, source_target_pairs={{0,96},{16,112},{32,0},{48,16},{64,32},{80,48},{96,64},{112,80},{1... | collective-permute-start | bytes 983048 | tf_op jit(solution)/shard_map/ppermute | solution.py:271
  112.6 0.3 fusion.2
  113.2 1.5 collective-permute-start.7
  114.8 7.9 %collective-permute-done.3 = bf16[8,96,128]{2,1,0:T(8,128)(2,1)S(1)} collective-permute-done((bf16[8,96,128]{2,1,0:T(8,128)(2,1)S(1)}, bf16[8,96,128]{2,1,0:T(8,128)(2,1)S(1)}, u32[]{:S(2)}, u32[]{:S(2)}) %collective-permute-start.3) | collective-permute-done | bytes 196640 | tf_op jit(solution)/shard_map/ppermute | solution.py:271
  122.8 3.5 %collective-permute-start.4 = (bf16[16,96,128]{2,1,0:T(8,128)(2,1)S(1)}, bf16[16,96,128]{2,1,0:T(8,128)(2,1)S(1)}, u32[]{:S(2)}, u32[]{:S(2)}) collective-permute-start(bf16[16,96,128]{2,1,0:T(8,128)(2,1)S(1)} %pad_maximum_fusion.2), channel_id=1, source_target_pairs={{0,96},{16,112},{32,0},{48,16},{64,32},{80,48},{96,64},{112,80},{1... | collective-permute-start | bytes 1179656 | tf_op jit(solution)/shard_map/ppermute | solution.py:271
  126.3 0.2 collective-permute-done.1
  126.7 0.2 add_convert_fusion.1
  126.9 5.8 %collective-permute-done.4 = bf16[16,96,128]{2,1,0:T(8,128)(2,1)S(1)} collective-permute-done((bf16[16,96,128]{2,1,0:T(8,128)(2,1)S(1)}, bf16[16,96,128]{2,1,0:T(8,128)(2,1)S(1)}, u32[]{:S(2)}, u32[]{:S(2)}) %collective-permute-start.4) | collective-permute-done | bytes 393248 | tf_op jit(solution)/shard_map/ppermute | solution.py:271
  132.7 3.5 %collective-permute-done.2 = bf16[16,96,128]{2,1,0:T(8,128)(2,1)S(1)} collective-permute-done((bf16[16,96,128]{2,1,0:T(8,128)(2,1)S(1)}, bf16[16,96,128]{2,1,0:T(8,128)(2,1)S(1)}, u32[]{:S(2)}, u32[]{:S(2)}) %collective-permute-start.2) | collective-permute-done | bytes 393248 | tf_op jit(solution)/shard_map/ppermute | solution.py:271
  136.2 0.2 add_convert_fusion
  136.5 14.4 %all_to_all.5 = bf16[16,176,128]{2,1,0:T(8,128)(2,1)S(1)} all-to-all(bf16[16,176,128]{2,1,0:T(8,128)(2,1)S(1)} %pad_maximum_fusion), channel_id=1, replica_groups=mesh['rep'=8,'graph'=16] {'graph'}, dimensions={0} | all-to-all | bytes 1441792 | tf_op jit(solution)/shard_map/all_to_all | solution.py:308
  151.0 21.5 %all-gather.1 = f32[1408,128]{1,0:T(8,128)S(1)} all-gather(f32[176,128]{1,0:T(8,128)S(1)} %convert_reduce_fusion), channel_id=3, replica_groups=mesh['rep'=8,'graph'=16] {'rep'}, dimensions={0}, use_global_device_ids=true | all-gather | bytes 811008 | tf_op jit(solution)/shard_map/all_gather | solution.py:309
  172.7 0.7 copy.23
  173.5 0.9 mul.54
  174.5 0.8 mul.59
  (62 shorter events, 1.8 us)
Async XLA Ops:
  7.2 68.2 %all-gather.4.cloned.1.call-start = ((), (), s32[]{:S(2)}) async-start(), calls=%async_computation.2 | async-start | bytes 6823936 | tf_op jit(solution)/shard_map/all_gather | solution.py:296
  7.9 167.4 %reduce-scatter.4.cloned.1.call-start = ((), (), s32[]{:S(2)}) async-start(), calls=%async_computation.3 | async-start | bytes 6823936
  8.6 2.2 %copy-start.8 = (bf16[640,2,640]{2,1,0:T(2,128)(2,1)S(1)}, bf16[640,2,640]{2,1,0:T(2,128)(2,1)}, u32[]{:S(2)}) copy-start(bf16[640,2,640]{2,1,0:T(2,128)(2,1)} %param.14) | copy-start | bytes 4915204
  10.8 0.7 copy-start.9
  10.8 0.7 copy-start.10
  10.9 1.4 copy-start
  10.9 1.5 copy-start.1
  10.9 1.6 copy-start.2
  47.2 1.9 %copy-start.3 = (bf16[1536,1280]{1,0:T(8,128)(2,1)}, bf16[1536,1280]{1,0:T(8,128)(2,1)S(1)}, u32[]{:S(2)}) copy-start(bf16[1536,1280]{1,0:T(8,128)(2,1)S(1)} %get-tuple-element.22.g1_hbm.g1_ref) | copy-start | bytes 11796484
  49.0 1.7 copy-start.5
  75.4 1.9 %copy-start.6 = (bf16[1280,1280]{1,0:T(8,128)(2,1)S(1)}, bf16[1280,1280]{1,0:T(8,128)(2,1)}, u32[]{:S(2)}) copy-start(bf16[1280,1280]{1,0:T(8,128)(2,1)} %copy-done.5) | copy-start | bytes 9830404
  77.3 18.1 %copy-start.4 = (bf16[1536,1280]{1,0:T(8,128)(2,1)S(1)}, bf16[1536,1280]{1,0:T(8,128)(2,1)}, u32[]{:S(2)}) copy-start(bf16[1536,1280]{1,0:T(8,128)(2,1)} %copy-done.3) | copy-start | bytes 11796484
  77.3 18.1 %copy-start.7 = (bf16[1280,1280]{1,0:T(8,128)(2,1)S(1)}, bf16[1280,1280]{1,0:T(8,128)(2,1)}, u32[]{:S(2)}) copy-start(bf16[1280,1280]{1,0:T(8,128)(2,1)} %copy-done.5) | copy-start | bytes 9830404
  99.6 3.4 %collective-permute-start.5 = (bf16[4,16,80,128]{3,2,1,0:T(8,128)(2,1)S(1)}, bf16[4,16,80,128]{3,2,1,0:T(8,128)(2,1)S(1)}, u32[]{:S(2)}, u32[]{:S(2)}) collective-permute-start(bf16[4,16,80,128]{3,2,1,0:T(8,128)(2,1)S(1)} %get-tuple-element.34), channel_id=1, source_target_pairs={{0,16},{16,0},{32,48},{48,32},{64,80},{80,64},{96,112},{112,96},{1... | collective-permute-start | bytes 3932168 | tf_op jit(solution)/shard_map/ppermute | solution.py:271
  100.3 12.3 %collective-permute-start = (bf16[4,16,96,128]{3,2,1,0:T(8,128)(2,1)S(1)}, bf16[4,16,96,128]{3,2,1,0:T(8,128)(2,1)S(1)}, u32[]{:S(2)}, u32[]{:S(2)}) collective-permute-start(bf16[4,16,96,128]{3,2,1,0:T(8,128)(2,1)S(1)} %get-tuple-element.26), channel_id=1, source_target_pairs={{0,16},{16,0},{32,48},{48,32},{64,80},{80,64},{96,112},{112,96},{1... | collective-permute-start | bytes 4718600 | tf_op jit(solution)/shard_map/ppermute | solution.py:271
  103.3 5.7 %collective-permute-start.8 = (bf16[8,80,128]{2,1,0:T(8,128)(2,1)S(1)}, bf16[8,80,128]{2,1,0:T(8,128)(2,1)S(1)}, u32[]{:S(2)}, u32[]{:S(2)}) collective-permute-start(bf16[8,80,128]{2,1,0:T(8,128)(2,1)S(1)} %get-tuple-element.47), channel_id=1, source_target_pairs={{0,96},{16,112},{32,0},{48,16},{64,32},{80,48},{96,64},{112,80},{1... | collective-permute-start | bytes 491528 | tf_op jit(solution)/shard_map/ppermute | solution.py:271
  105.8 7.3 %collective-permute-start.6 = (bf16[8,80,128]{2,1,0:T(8,128)(2,1)S(1)}, bf16[8,80,128]{2,1,0:T(8,128)(2,1)S(1)}, u32[]{:S(2)}, u32[]{:S(2)}) collective-permute-start(bf16[8,80,128]{2,1,0:T(8,128)(2,1)S(1)} %get-tuple-element.46), channel_id=1, source_target_pairs={{0,32},{16,48},{32,64},{48,80},{64,96},{80,112},{96,0},{112,16},{1... | collective-permute-start | bytes 491528 | tf_op jit(solution)/shard_map/ppermute | solution.py:271
  109.0 17.7 %collective-permute-start.9 = (bf16[16,80,128]{2,1,0:T(8,128)(2,1)S(1)}, bf16[16,80,128]{2,1,0:T(8,128)(2,1)S(1)}, u32[]{:S(2)}, u32[]{:S(2)}) collective-permute-start(bf16[16,80,128]{2,1,0:T(8,128)(2,1)S(1)} %pad_maximum_fusion.4), channel_id=1, source_target_pairs={{0,96},{16,112},{32,0},{48,16},{64,32},{80,48},{96,64},{112,80},{1... | collective-permute-start | bytes 983048 | tf_op jit(solution)/shard_map/ppermute | solution.py:271
  113.0 9.8 %collective-permute-start.3 = (bf16[8,96,128]{2,1,0:T(8,128)(2,1)S(1)}, bf16[8,96,128]{2,1,0:T(8,128)(2,1)S(1)}, u32[]{:S(2)}, u32[]{:S(2)}) collective-permute-start(bf16[8,96,128]{2,1,0:T(8,128)(2,1)S(1)} %get-tuple-element.45), channel_id=1, source_target_pairs={{0,96},{16,112},{32,0},{48,16},{64,32},{80,48},{96,64},{112,80},{1... | collective-permute-start | bytes 589832 | tf_op jit(solution)/shard_map/ppermute | solution.py:271
  113.2 13.6 %collective-permute-start.7 = (bf16[16,80,128]{2,1,0:T(8,128)(2,1)S(1)}, bf16[16,80,128]{2,1,0:T(8,128)(2,1)S(1)}, u32[]{:S(2)}, u32[]{:S(2)}) collective-permute-start(bf16[16,80,128]{2,1,0:T(8,128)(2,1)S(1)} %pad_maximum_fusion.3), channel_id=1, source_target_pairs={{0,32},{16,48},{32,64},{48,80},{64,96},{80,112},{96,0},{112,16},{1... | collective-permute-start | bytes 983048 | tf_op jit(solution)/shard_map/ppermute | solution.py:271
  114.7 11.8 %collective-permute-start.1 = (bf16[8,96,128]{2,1,0:T(8,128)(2,1)S(1)}, bf16[8,96,128]{2,1,0:T(8,128)(2,1)S(1)}, u32[]{:S(2)}, u32[]{:S(2)}) collective-permute-start(bf16[8,96,128]{2,1,0:T(8,128)(2,1)S(1)} %get-tuple-element.44), channel_id=1, source_target_pairs={{0,32},{16,48},{32,64},{48,80},{64,96},{80,112},{96,0},{112,16},{1... | collective-permute-start | bytes 589832 | tf_op jit(solution)/shard_map/ppermute | solution.py:271
  122.8 9.9 %collective-permute-start.4 = (bf16[16,96,128]{2,1,0:T(8,128)(2,1)S(1)}, bf16[16,96,128]{2,1,0:T(8,128)(2,1)S(1)}, u32[]{:S(2)}, u32[]{:S(2)}) collective-permute-start(bf16[16,96,128]{2,1,0:T(8,128)(2,1)S(1)} %pad_maximum_fusion.2), channel_id=1, source_target_pairs={{0,96},{16,112},{32,0},{48,16},{64,32},{80,48},{96,64},{112,80},{1... | collective-permute-start | bytes 1179656 | tf_op jit(solution)/shard_map/ppermute | solution.py:271
  126.6 9.6 %collective-permute-start.2 = (bf16[16,96,128]{2,1,0:T(8,128)(2,1)S(1)}, bf16[16,96,128]{2,1,0:T(8,128)(2,1)S(1)}, u32[]{:S(2)}, u32[]{:S(2)}) collective-permute-start(bf16[16,96,128]{2,1,0:T(8,128)(2,1)S(1)} %pad_maximum_fusion.1), channel_id=1, source_target_pairs={{0,32},{16,48},{32,64},{48,80},{64,96},{80,112},{96,0},{112,16},{1... | collective-permute-start | bytes 1179656 | tf_op jit(solution)/shard_map/ppermute | solution.py:271
Sparse Core Ops, SparseCore 0:
  10.2 65.1 all-gather.3
  79.4 83.6 reduce-scatter.3
where the time goes:
time: 182 us
  Pallas kernels  56.9 us (31%)
  waiting for transfers between devices  48.3 us (27%)
  blocking collectives  35.9 us (20%)
  between operations  15 us (8%)
  starting transfers between devices  12.3 us (7%)
  local copies, waits for them, and re-layouts  12 us (7%)
    pallas_call x1, Pallas kernels, grads(): pl.pallas_call(grad_kernel, out_shape=(S((k0, edges), BF16), S((2 * k1, 2...  34.7 us
    all_gather x1, waiting for transfers between devices, per_device(): lax.all_gather(node_feats.transpose(1, 0, 2), 'graph', axis=0, tiled=False)  24.6 us
    ppermute x10, waiting for transfers between devices, send_rep(): return lax.ppermute(value, 'rep', rep_shift(dx, dc))  23 us
    all_gather x1, blocking collectives, per_device(): lax.all_gather(pieces.astype(F32).sum(0), 'rep', axis=0, tiled=False)  21.5 us
    pallas_call x1, Pallas kernels, first_weights(): pl.pallas_call(first_kernel, out_shape=(S((k0, edges), BF16), S((k1, 2 *...  18 us
    all_to_all x1, blocking collectives, per_device(): lax.all_to_all(jnp.concatenate([first, second], axis=1), 'graph', split_a...  14.4 us
    ppermute x10, starting transfers between devices, send_rep(): return lax.ppermute(value, 'rep', rep_shift(dx, dc))  12.3 us
    unnamed x24, local copies, waits for them, and re-layouts  9.24 us
  transfers between devices with their start and end apart: 12, of which 7 were waited for; matrix products, arithmetic and copies ran while one was open for 4% of the time, Pallas kernels for 31%

commit v1 on v0

--- a/solution.py
+++ b/solution.py
@@ -278,15 +278,35 @@
     return total.astype(BF16)
 
 
-def sum_over_rep(mine, theirs):
+def pass_kernel(*refs):
+    pass
+
+
+def once(value, after):
+    return pl.pallas_call(
+        pass_kernel, out_shape=S(value.shape, value.dtype), in_specs=[VM] * 2, out_specs=VM,
+        input_output_aliases={0: 0}, compiler_params=pltpu.CompilerParams(vmem_limit_bytes=8 << 20), name="once",
+    )(value, after[(0,) * (after.ndim - 2)][:16])
+
+
+def over_cores(mine, theirs):
     got = send_rep(theirs, 0, 1)
-    r = [add(mine[k], got[k]) for k in range(4)]
-    half = r[2].shape[0] // 2
-    up = send_rep(r[2][:half], 1, 0)
-    down = send_rep(r[2][half:], -1, 0)
-    r1 = jnp.concatenate([add(r[1][:half], up), r[1][half:]])
-    r3 = jnp.concatenate([r[3][:half], add(r[3][half:], down)])
-    return add(r[0], send_rep(r1, 1, 0), send_rep(r3, -1, 0))
+    far = add(mine[2], got[2])
+    half = far.shape[0] // 2
+    return got, far[:half], far[half:]
+
+
+def first_step(mine, got, low, high):
+    up = send_rep(low, 1, 0)
+    down = send_rep(high, -1, 0)
+    half = up.shape[0]
+    to_up = jnp.concatenate([add(mine[1][:half], got[1][:half], up), add(mine[1][half:], got[1][half:])])
+    to_down = jnp.concatenate([add(mine[3][:half], got[3][:half]), add(mine[3][half:], got[3][half:], down)])
+    return to_up, to_down
+
+
+def last_step(mine, got, to_up, to_down):
+    return add(mine[0], got[0], send_rep(to_up, 1, 0), send_rep(to_down, -1, 0))
 
 
 def per_device(node_feats, grad_out, wigner, w0, w1, w2, edge_source, edge_target, edge_count):
@@ -302,9 +322,13 @@
     rep = lax.axis_index("rep")
     place = jnp.stack([rep // 2, rep % 2])
     v0, v1, v2, *mine, theirs = first_weights(place, x, wigner, src, g0, g1, g2)
-    first = sum_over_rep(mine, theirs)
-    *mine, theirs = second_weights(place, v0, v1, v2, g0, g1, g2, parts)
-    second = sum_over_rep(mine, theirs)
+    got, low, high = over_cores(mine, theirs)
+    *mine2, theirs2 = second_weights(place, v0, v1, v2, g0, g1, g2, parts)
+    got2, low2, high2 = over_cores(mine2, once(theirs2, got))
+    to_up, to_down = first_step(mine, got, low, high)
+    to_up2, to_down2 = first_step(mine2, got2, low2, high2)
+    first = last_step(mine, got, to_up, to_down)
+    second = last_step(mine2, got2, to_up2, to_down2)
     pieces = lax.all_to_all(jnp.concatenate([first, second], axis=1), "graph", split_axis=0, concat_axis=0, tiled=True)
     whole = lax.all_gather(pieces.astype(F32).sum(0), "rep", axis=0, tiled=False)
     first = whole[:, :FIRST_ROWS].reshape(-1, C)

time: 182 us -> 172 us (0.945)
  waiting for transfers between devices: 48.3 us -> 42.8 us
  blocking collectives: 35.9 us -> 32.4 us
    ppermute x10, waiting for transfers between devices: 23 us -> 17.5 us  [send_rep(): return lax.ppermute(value, 'rep', rep_shift(dx, dc))]
    all_gather x1, blocking collectives: 21.5 us -> 17.6 us  [per_device(): lax.all_gather(pieces.astype(F32).sum(0), 'rep', axis=0, tiled=False)]
  transfers between devices with their start and end apart: 12 -> 12, of which waited for: 7 -> 5; matrix products, arithmetic and copies ran while one was open for 4% -> 4% of each run, Pallas kernels for 31% -> 33%
where the time goes in v1:
time: 172 us; the launch traced here: 171 us
  Pallas kernels  56.9 us (33%)
  waiting for transfers between devices  42.8 us (25%)
  blocking collectives  32.4 us (19%)
  between operations  15 us (9%)
  local copies, waits for them, and re-layouts  11.9 us (7%)
  starting transfers between devices  10.9 us (6%)
    pallas_call x1, Pallas kernels, grads(): pl.pallas_call(grad_kernel, out_shape=(S((k0, edges), BF16), S((2 * k1, 2...  34.7 us
    all_gather x1, waiting for transfers between devices, per_device(): lax.all_gather(node_feats.transpose(1, 0, 2), 'graph', axis=0, tiled=False)  24.6 us
    pallas_call x1, Pallas kernels, first_weights(): pl.pallas_call(first_kernel, out_shape=(S((k0, edges), BF16), S((k1, 2 *...  18 us
    all_gather x1, blocking collectives, per_device(): lax.all_gather(pieces.astype(F32).sum(0), 'rep', axis=0, tiled=False)  17.6 us
    ppermute x10, waiting for transfers between devices, send_rep(): return lax.ppermute(value, 'rep', rep_shift(dx, dc))  17.5 us
    all_to_all x1, blocking collectives, per_device(): lax.all_to_all(jnp.concatenate([first, second], axis=1), 'graph', split_a...  14.8 us
    ppermute x10, starting transfers between devices, send_rep(): return lax.ppermute(value, 'rep', rep_shift(dx, dc))  10.8 us
    unnamed x24, local copies, waits for them, and re-layouts  9.24 us
  transfers between devices with their start and end apart: 12, of which 5 were waited for; matrix products, arithmetic and copies ran while one was open for 4% of the time, Pallas kernels for 33%

profile of v1, /device:TPU:1, one launch (start us, length us, event | category | flops | bytes accessed | tf_op | source)
XLA Modules:
  0.0 171.4 jit_solution(7641705440295148806)
XLA Ops:
  7.2 0.7 all-gather.4.cloned.1.call-update
  8.6 2.2 %copy.21 = bf16[96,8,2,768]{3,1,2,0:T(8,128)(2,1)S(1)} copy(bf16[96,8,2,768]{3,2,1,0:T(2,128)(2,1)} %bitcast.96) | data formatting | bytes 4718592
  10.9 0.3 copy.22
  11.2 0.4 copy-done.9
  11.5 0.7 copy-done
  12.4 34.7 %grads.1 = (bf16[896,640]{1,0:T(8,128)(2,1)S(1)}, bf16[1536,1280]{1,0:T(8,128)(2,1)S(1)}, bf16[1280,1280]{1,0:T(8,128)(2,1)S(1)}, bf16[16,49,32,128]{3,2,1,0:T(8,128)(2,1)}) custom-call(s32[1]{0:T(128)S(6)} %copy.26.count_ref, bf16[49,32,128]{2,1,0:T(8,128)(2,1)S(1)} %bitcast.93, bf16[235,640]{1,0:T(8,128)(2,1)S(1)} %copy-done.2, ...), custom_call_target="tpu_custom_call" | custom-call | tf_op jit(solution)/shard_map/grads/pallas_call | solution.py:210
  47.2 1.9 %copy-done.3 = bf16[1536,1280]{1,0:T(8,128)(2,1)} copy-done((bf16[1536,1280]{1,0:T(8,128)(2,1)}, bf16[1536,1280]{1,0:T(8,128)(2,1)S(1)}, u32[]{:S(2)}) %copy-start.3) | copy-done | bytes 3932184
  49.0 1.7 copy-done.5
  50.8 24.6 %all-gather.4.cloned.1.call-done = bf16[784,32,128]{2,1,0:T(8,128)(2,1)} async-done(((bf16[49,32,128]{2,1,0:T(8,128)(2,1)}), bf16[784,32,128]{2,1,0:T(8,128)(2,1)}) %all-gather.4.cloned.1.call-update) | async-done | bytes 6422544 | tf_op jit(solution)/shard_map/all_gather | solution.py:316
  75.4 1.9 %copy-done.6 = bf16[1280,1280]{1,0:T(8,128)(2,1)S(1)} copy-done((bf16[1280,1280]{1,0:T(8,128)(2,1)S(1)}, bf16[1280,1280]{1,0:T(8,128)(2,1)}, u32[]{:S(2)}) %copy-start.6) | copy-done | bytes 3276824
  77.3 18.0 %first_weights.1 = (bf16[896,640]{1,0:T(8,128)(2,1)S(1)}, bf16[768,1280]{1,0:T(8,128)(2,1)S(1)}, bf16[640,1280]{1,0:T(8,128)(2,1)S(1)}, bf16[16,96,128]{2,1,0:T(...) custom-call(s32[2]{0:T(128)S(1)} %pad_add_fusion.place_ref, ...), custom_call_target="tpu_custom_call" | custom-call | flops 10000000000 | bytes 20000000 | tf_op jit(solution)/shard_map/first_weights/pallas_call | solution.py:234
  95.4 0.8 collective-permute-start
  96.1 4.1 %second_weights.1 = (bf16[16,80,128]{2,1,0:T(8,128)(2,1)S(1)}, bf16[16,80,128]{2,1,0:T(8,128)(2,1)S(1)}, bf16[16,80,128]{2,1,0:T(8,128)(2,1)S(1)}, bf16[16,80,12...) custom-call(s32[2]{0:T(128)S(1)} %pad_add_fusion.place_ref, bf16[896,640]{1,0:T(8,128)(2,1)S(1)} %get-tuple-element.30.v0_ref, ...), custom_call_target="tpu_custom_call" | custom-call | flops 4000000000 | bytes 10000000 | tf_op jit(solution)/shard_map/second_weights/pallas_call | solution.py:250
  100.6 1.3 collective-permute-start.1
  101.8 1.5 collective-permute-start.3
  103.3 4.5 %collective-permute-done.1 = bf16[8,96,128]{2,1,0:T(8,128)(2,1)S(1)} collective-permute-done((bf16[8,96,128]{2,1,0:T(8,128)(2,1)S(1)}, bf16[8,96,128]{2,1,0:T(8,128)(2,1)S(1)}, u32[]{:S(2)}, u32[]{:S(2)}) %collective-permute-start.1) | collective-permute-done | bytes 196640 | tf_op jit(solution)/shard_map/ppermute | solution.py:271
  107.9 0.3 fusion.13
  108.3 1.0 collective-permute-start.6
  109.3 1.8 %collective-permute-start.8 = (bf16[8,80,128]{2,1,0:T(8,128)(2,1)S(1)}, bf16[8,80,128]{2,1,0:T(8,128)(2,1)S(1)}, u32[]{:S(2)}, u32[]{:S(2)}) collective-permute-start(bf16[8,80,128]{2,1,0:T(8,128)(2,1)S(1)} %get-tuple-element.53), channel_id=1, source_target_pairs={{0,96},{16,112},{32,0},{48,16},{64,32},{80,48},{96,64},{112,80},{1... | collective-permute-start | bytes 491528 | tf_op jit(solution)/shard_map/ppermute | solution.py:271
  111.1 1.2 collective-permute-start.4
  112.3 0.4 collective-permute-start.2
  112.7 1.4 collective-permute-done.6
  114.1 0.3 fusion.19
  114.4 2.7 %collective-permute-start.9 = (bf16[16,80,128]{2,1,0:T(8,128)(2,1)S(1)}, bf16[16,80,128]{2,1,0:T(8,128)(2,1)S(1)}, u32[]{:S(2)}, u32[]{:S(2)}) collective-permute-start(bf16[16,80,128]{2,1,0:T(8,128)(2,1)S(1)} %pad_maximum_fusion.4), channel_id=1, source_target_pairs={{0,96},{16,112},{32,0},{48,16},{64,32},{80,48},{96,64},{112,80},{1... | collective-permute-start | bytes 983048 | tf_op jit(solution)/shard_map/ppermute | solution.py:271
  117.3 4.7 %collective-permute-done.4 = bf16[16,96,128]{2,1,0:T(8,128)(2,1)S(1)} collective-permute-done((bf16[16,96,128]{2,1,0:T(8,128)(2,1)S(1)}, bf16[16,96,128]{2,1,0:T(8,128)(2,1)S(1)}, u32[]{:S(2)}, u32[]{:S(2)}) %collective-permute-start.4) | collective-permute-done | bytes 393248 | tf_op jit(solution)/shard_map/ppermute | solution.py:271
  122.0 0.2 fusion.3
  122.2 6.8 %collective-permute-done.9 = bf16[16,80,128]{2,1,0:T(8,128)(2,1)S(1)} collective-permute-done((bf16[16,80,128]{2,1,0:T(8,128)(2,1)S(1)}, bf16[16,80,128]{2,1,0:T(8,128)(2,1)S(1)}, u32[]{:S(2)}, u32[]{:S(2)}) %collective-permute-start.9) | collective-permute-done | bytes 327712 | tf_op jit(solution)/shard_map/ppermute | solution.py:271
  129.3 14.8 %all_to_all.5 = bf16[16,176,128]{2,1,0:T(8,128)(2,1)S(1)} all-to-all(bf16[16,176,128]{2,1,0:T(8,128)(2,1)S(1)} %pad_maximum_fusion), channel_id=1, replica_groups=mesh['rep'=8,'graph'=16] {'graph'}, dimensions={0} | all-to-all | bytes 1441792 | tf_op jit(solution)/shard_map/all_to_all | solution.py:332
  144.2 17.6 %all-gather.1 = f32[1408,128]{1,0:T(8,128)S(1)} all-gather(f32[176,128]{1,0:T(8,128)S(1)} %convert_reduce_fusion), channel_id=3, replica_groups=mesh['rep'=8,'graph'=16] {'rep'}, dimensions={0}, use_global_device_ids=true | all-gather | bytes 811008 | tf_op jit(solution)/shard_map/all_gather | solution.py:333
  162.0 0.7 copy.24
  162.8 0.9 mul.54
  163.8 0.8 mul.59
  (58 shorter events, 1.6 us)
Async XLA Ops:
  7.2 68.2 %all-gather.4.cloned.1.call-start = ((), (), s32[]{:S(2)}) async-start(), calls=%async_computation.2 | async-start | bytes 6823936 | tf_op jit(solution)/shard_map/all_gather | solution.py:316
  7.9 156.7 %reduce-scatter.4.cloned.1.call-start = ((), (), s32[]{:S(2)}) async-start(), calls=%async_computation.3 | async-start | bytes 6823936
  8.6 2.2 %copy-start.8 = (bf16[640,2,640]{2,1,0:T(2,128)(2,1)S(1)}, bf16[640,2,640]{2,1,0:T(2,128)(2,1)}, u32[]{:S(2)}) copy-start(bf16[640,2,640]{2,1,0:T(2,128)(2,1)} %param.14) | copy-start | bytes 4915204
  10.8 0.7 copy-start.9
  10.8 0.7 copy-start.10
  10.9 1.4 copy-start
  10.9 1.5 copy-start.1
  10.9 1.6 copy-start.2
  47.2 1.9 %copy-start.3 = (bf16[1536,1280]{1,0:T(8,128)(2,1)}, bf16[1536,1280]{1,0:T(8,128)(2,1)S(1)}, u32[]{:S(2)}) copy-start(bf16[1536,1280]{1,0:T(8,128)(2,1)S(1)} %get-tuple-element.22.g1_hbm.g1_ref) | copy-start | bytes 11796484
  49.0 1.7 copy-start.5
  75.4 1.9 %copy-start.6 = (bf16[1280,1280]{1,0:T(8,128)(2,1)S(1)}, bf16[1280,1280]{1,0:T(8,128)(2,1)}, u32[]{:S(2)}) copy-start(bf16[1280,1280]{1,0:T(8,128)(2,1)} %copy-done.5) | copy-start | bytes 9830404
  77.3 18.8 %copy-start.4 = (bf16[1536,1280]{1,0:T(8,128)(2,1)S(1)}, bf16[1536,1280]{1,0:T(8,128)(2,1)}, u32[]{:S(2)}) copy-start(bf16[1536,1280]{1,0:T(8,128)(2,1)} %copy-done.3) | copy-start | bytes 11796484
  77.3 18.8 %copy-start.7 = (bf16[1280,1280]{1,0:T(8,128)(2,1)S(1)}, bf16[1280,1280]{1,0:T(8,128)(2,1)}, u32[]{:S(2)}) copy-start(bf16[1280,1280]{1,0:T(8,128)(2,1)} %copy-done.5) | copy-start | bytes 9830404
  95.4 4.9 %collective-permute-start = (bf16[4,16,96,128]{3,2,1,0:T(8,128)(2,1)S(1)}, bf16[4,16,96,128]{3,2,1,0:T(8,128)(2,1)S(1)}, u32[]{:S(2)}, u32[]{:S(2)}) collective-permute-start(bf16[4,16,96,128]{3,2,1,0:T(8,128)(2,1)S(1)} %get-tuple-element.26), channel_id=1, source_target_pairs={{0,16},{16,0},{32,48},{48,32},{64,80},{80,64},{96,112},{112,96},{1... | collective-permute-start | bytes 4718600 | tf_op jit(solution)/shard_map/ppermute | solution.py:271
  100.3 7.8 %collective-permute-start.5 = (bf16[4,16,80,128]{3,2,1,0:T(8,128)(2,1)S(1)}, bf16[4,16,80,128]{3,2,1,0:T(8,128)(2,1)S(1)}, u32[]{:S(2)}, u32[]{:S(2)}) collective-permute-start(bf16[4,16,80,128]{3,2,1,0:T(8,128)(2,1)S(1)} %once.1), channel_id=1, source_target_pairs={{0,16},{16,0},{32,48},{48,32},{64,80},{80,64},{96,112},{112,96},{1... | collective-permute-start | bytes 3932168 | tf_op jit(solution)/shard_map/ppermute | solution.py:271
  100.6 7.3 %collective-permute-start.1 = (bf16[8,96,128]{2,1,0:T(8,128)(2,1)S(1)}, bf16[8,96,128]{2,1,0:T(8,128)(2,1)S(1)}, u32[]{:S(2)}, u32[]{:S(2)}) collective-permute-start(bf16[8,96,128]{2,1,0:T(8,128)(2,1)S(1)} %get-tuple-element.50), channel_id=1, source_target_pairs={{0,32},{16,48},{32,64},{48,80},{64,96},{80,112},{96,0},{112,16},{1... | collective-permute-start | bytes 589832 | tf_op jit(solution)/shard_map/ppermute | solution.py:271
  101.8 6.0 %collective-permute-start.3 = (bf16[8,96,128]{2,1,0:T(8,128)(2,1)S(1)}, bf16[8,96,128]{2,1,0:T(8,128)(2,1)S(1)}, u32[]{:S(2)}, u32[]{:S(2)}) collective-permute-start(bf16[8,96,128]{2,1,0:T(8,128)(2,1)S(1)} %get-tuple-element.51), channel_id=1, source_target_pairs={{0,96},{16,112},{32,0},{48,16},{64,32},{80,48},{96,64},{112,80},{1... | collective-permute-start | bytes 589832 | tf_op jit(solution)/shard_map/ppermute | solution.py:271
  108.3 5.8 %collective-permute-start.6 = (bf16[8,80,128]{2,1,0:T(8,128)(2,1)S(1)}, bf16[8,80,128]{2,1,0:T(8,128)(2,1)S(1)}, u32[]{:S(2)}, u32[]{:S(2)}) collective-permute-start(bf16[8,80,128]{2,1,0:T(8,128)(2,1)S(1)} %get-tuple-element.52), channel_id=1, source_target_pairs={{0,32},{16,48},{32,64},{48,80},{64,96},{80,112},{96,0},{112,16},{1... | collective-permute-start | bytes 491528 | tf_op jit(solution)/shard_map/ppermute | solution.py:271
  109.3 4.9 %collective-permute-start.8 = (bf16[8,80,128]{2,1,0:T(8,128)(2,1)S(1)}, bf16[8,80,128]{2,1,0:T(8,128)(2,1)S(1)}, u32[]{:S(2)}, u32[]{:S(2)}) collective-permute-start(bf16[8,80,128]{2,1,0:T(8,128)(2,1)S(1)} %get-tuple-element.53), channel_id=1, source_target_pairs={{0,96},{16,112},{32,0},{48,16},{64,32},{80,48},{96,64},{112,80},{1... | collective-permute-start | bytes 491528 | tf_op jit(solution)/shard_map/ppermute | solution.py:271
  111.1 11.0 %collective-permute-start.4 = (bf16[16,96,128]{2,1,0:T(8,128)(2,1)S(1)}, bf16[16,96,128]{2,1,0:T(8,128)(2,1)S(1)}, u32[]{:S(2)}, u32[]{:S(2)}) collective-permute-start(bf16[16,96,128]{2,1,0:T(8,128)(2,1)S(1)} %pad_maximum_fusion.2), channel_id=1, source_target_pairs={{0,96},{16,112},{32,0},{48,16},{64,32},{80,48},{96,64},{112,80},{1... | collective-permute-start | bytes 1179656 | tf_op jit(solution)/shard_map/ppermute | solution.py:271
  112.3 9.7 %collective-permute-start.2 = (bf16[16,96,128]{2,1,0:T(8,128)(2,1)S(1)}, bf16[16,96,128]{2,1,0:T(8,128)(2,1)S(1)}, u32[]{:S(2)}, u32[]{:S(2)}) collective-permute-start(bf16[16,96,128]{2,1,0:T(8,128)(2,1)S(1)} %pad_maximum_fusion.1), channel_id=1, source_target_pairs={{0,32},{16,48},{32,64},{48,80},{64,96},{80,112},{96,0},{112,16},{1... | collective-permute-start | bytes 1179656 | tf_op jit(solution)/shard_map/ppermute | solution.py:271
  114.4 14.6 %collective-permute-start.9 = (bf16[16,80,128]{2,1,0:T(8,128)(2,1)S(1)}, bf16[16,80,128]{2,1,0:T(8,128)(2,1)S(1)}, u32[]{:S(2)}, u32[]{:S(2)}) collective-permute-start(bf16[16,80,128]{2,1,0:T(8,128)(2,1)S(1)} %pad_maximum_fusion.4), channel_id=1, source_target_pairs={{0,96},{16,112},{32,0},{48,16},{64,32},{80,48},{96,64},{112,80},{1... | collective-permute-start | bytes 983048 | tf_op jit(solution)/shard_map/ppermute | solution.py:271
  117.2 11.8 %collective-permute-start.7 = (bf16[16,80,128]{2,1,0:T(8,128)(2,1)S(1)}, bf16[16,80,128]{2,1,0:T(8,128)(2,1)S(1)}, u32[]{:S(2)}, u32[]{:S(2)}) collective-permute-start(bf16[16,80,128]{2,1,0:T(8,128)(2,1)S(1)} %pad_maximum_fusion.3), channel_id=1, source_target_pairs={{0,32},{16,48},{32,64},{48,80},{64,96},{80,112},{96,0},{112,16},{1... | collective-permute-start | bytes 983048 | tf_op jit(solution)/shard_map/ppermute | solution.py:271
Sparse Core Ops, SparseCore 0:
  10.2 65.1 all-gather.3
  79.4 84.3 reduce-scatter.3
